TPU v7x, 32 devices: a whole 2x2x4 slice. The times are simulated.
32 devices in a mesh: band: 8 (over z, y), chan: 4 (over x, core).
Axes of the slice: x: 2, y: 2, z: 4, core: 2. Of those that a mesh axis runs over, the one named last changes fastest.
Arguments:
- new_frames: bfloat16 [4, 32, 512, 320], P(None, 'band', 'chan'), may hold values from -6 to 6
- cached_frames: bfloat16 [2, 32, 512, 320], P(None, 'band', 'chan'), may hold values from -6 to 6
- conv_weight: bfloat16 [3, 3, 3, 512, 512], P(None, None, None, 'chan'), may hold values from -0.0546875 to 0.0546875
- out_bias: float32 [512], P('chan'), may hold values from -3 to 3
Outputs:
- conv_out: bfloat16 [4, 32, 512, 320], P(None, 'band', 'chan')
All inputs are finite; a program needn't handle non-finite values.
Results may differ from a plain program's by a relative error of at most 0.001.
Values may be sent and summed in bfloat16 or wider, within the bound.
A program may use at most 128 MiB of HBM per device.

v0:
```python
import jax
import jax.numpy as jnp
from jax import lax
from jax.sharding import PartitionSpec as P


def with_halo(block, sides, width):
    for axis, dim in sides:
        count = lax.axis_size(axis)
        forward = [(i, i + 1) for i in range(count - 1)]
        backward = [(target, source) for source, target in forward]
        low = lax.ppermute(
            lax.slice_in_dim(block, block.shape[dim] - width, None, axis=dim), axis, forward
        )
        high = lax.ppermute(lax.slice_in_dim(block, 0, width, axis=dim), axis, backward)
        block = jnp.concatenate([low, block, high], axis=dim)
    return block


def convolve(padded, kernel):
    frame_count = padded.shape[0] - 2
    row_count = padded.shape[1] - 2
    col_count = padded.shape[3] - 2
    summed = jnp.zeros((frame_count, row_count, kernel.shape[3], col_count), jnp.float32)
    for time_tap in range(3):
        for row_tap in range(3):
            window = padded[time_tap : time_tap + frame_count, row_tap : row_tap + row_count]
            products = jnp.einsum(
                "kdc,frcw->kfrdw",
                kernel[time_tap, row_tap],
                window,
                preferred_element_type=jnp.float32,
            )
            summed = (
                summed
                + products[0, :, :, :, 0:col_count]
                + products[1, :, :, :, 1 : col_count + 1]
                + products[2, :, :, :, 2 : col_count + 2]
            )
    return summed


def pad_columns(layered):
    return jnp.pad(layered, ((0, 0), (0, 0), (0, 0), (1, 1)))


def on_device(new_frames, cached_frames, conv_weight, out_bias):
    stacked = jnp.concatenate([cached_frames, new_frames], axis=0)
    rimmed = with_halo(stacked, (("band", 1),), 1)
    summed = convolve(pad_columns(lax.all_gather(rimmed, "chan", axis=2, tiled=True)), conv_weight)
    return (summed + out_bias[None, None, :, None]).astype(jnp.bfloat16)


def solution(mesh):
    in_specs = (
        P(None, "band", "chan", None),
        P(None, "band", "chan", None),
        P(None, None, None, "chan", None),
        P("chan"),
    )
    out_specs = P(None, "band", "chan", None)
    return jax.shard_map(
        on_device, mesh=mesh, in_specs=in_specs, out_specs=out_specs, check_vma=False
    )
```

profile of v0, /device:TPU:0, one launch (start us, length us, event | category | flops | bytes accessed | tf_op | source)
XLA Modules:
  0.0 195.8 jit_solution(729754602605033994)
XLA Ops:
  6.5 0.0 all-gather.2.cloned.1.call-start
  6.5 1.1 constant_dynamic-update-slice_fusion.1
  7.7 1.5 constant_dynamic-update-slice_fusion
  9.2 0.1 fusion.105
  9.2 4.9 %collective-permute-start = (bf16[6,1,128,320]{2,3,1,0:T(8,128)(2,1)S(1)}, bf16[6,1,128,320]{2,3,1,0:T(8,128)(2,1)S(1)}, u32[]{:S(2)}, u32[]{:S(2)}) collective-permute-start(bf16[6,1,128,320]{2,3,1,0:T(8,128)(2,1)S(1)} %get-tuple-element.5), channel_id=1, source_target_pairs={{0,4},{4,8},{8,12},{12,16},{16,20},{20,24},{24,28},{1,5},{5,9},{9,... | collective-permute-start | bytes 1474568 | tf_op jit(solution)/shard_map/ppermute | solution.py:12
  14.2 0.0 copy-start.1
  14.2 1.6 collective-permute-start.1
  15.7 19.4 %collective-permute-done = bf16[6,1,128,320]{2,3,1,0:T(8,128)(2,1)S(1)} collective-permute-done((bf16[6,1,128,320]{2,3,1,0:T(8,128)(2,1)S(1)}, bf16[6,1,128,320]{2,3,1,0:T(8,128)(2,1)S(1)}, u32[]{:S(2)}, u32[]{:S(2)}) %collective-permute-start) | collective-permute-done | bytes 491552 | tf_op jit(solution)/shard_map/ppermute | solution.py:12
  35.1 0.0 collective-permute-done.1
  35.1 2.0 pad_maximum_fusion
  37.1 0.0 all-gather.2.cloned.1.call-update
  37.1 81.5 %all-gather.2.cloned.1.call-done = bf16[6,6,512,320]{2,3,1,0:T(8,128)(2,1)} async-done(((bf16[6,6,128,320]{2,3,1,0:T(8,128)(2,1)}), bf16[6,6,512,320]{2,3,1,0:T(8,128)(2,1)}) %all-gather.2.cloned.1.call-update) | async-done | bytes 11796496 | tf_op jit(solution)/shard_map/all_gather | solution.py:50
  118.6 0.0 copy-done.1
  118.6 9.0 %fusion.42 = f32[3,4,4,128,322]{3,4,0,2,1:T(8,128)} fusion(bf16[6,6,512,320]{2,3,1,0:T(8,128)(2,1)} %all-gather.2.cloned.1.call-done, bf16[3,3,3,128,512]{4,3,2,1,0:T(8,128)(2,1)S(1)} %copy-done.1), kind=kOutput, calls=%fused_computation.32 | convolution fusion | flops 2025848832 | bytes 20103168 | tf_op jit(solution)/shard_map/kdc,frcw->kfrdw/dot_general | solution.py:28
  127.7 0.0 copy-done
  127.7 5.3 %fusion.45 = f32[3,4,4,128,322]{3,4,0,2,1:T(8,128)} fusion(bf16[6,6,512,320]{2,3,1,0:T(8,128)(2,1)S(1)} %copy-done, bf16[3,3,3,128,512]{4,3,2,1,0:T(8,128)(2,1)S(1)} %copy-done.1), kind=kOutput, calls=%fused_computation.33 | convolution fusion | flops 2025848832 | bytes 20103168 | tf_op jit(solution)/shard_map/kdc,frcw->kfrdw/dot_general | solution.py:28
  133.0 5.1 %fusion.48 = f32[3,4,4,128,322]{3,4,0,2,1:T(8,128)} fusion(bf16[6,6,512,320]{2,3,1,0:T(8,128)(2,1)S(1)} %copy-done, bf16[3,3,3,128,512]{4,3,2,1,0:T(8,128)(2,1)S(1)} %copy-done.1), kind=kOutput, calls=%fused_computation.34 | convolution fusion | flops 2025848832 | bytes 20103168 | tf_op jit(solution)/shard_map/kdc,frcw->kfrdw/dot_general | solution.py:28
  138.1 5.2 %fusion.51 = f32[3,4,4,128,322]{3,4,0,2,1:T(8,128)} fusion(bf16[6,6,512,320]{2,3,1,0:T(8,128)(2,1)S(1)} %copy-done, bf16[3,3,3,128,512]{4,3,2,1,0:T(8,128)(2,1)S(1)} %copy-done.1), kind=kOutput, calls=%fused_computation.35 | convolution fusion | flops 2025848832 | bytes 20103168 | tf_op jit(solution)/shard_map/kdc,frcw->kfrdw/dot_general | solution.py:28
  143.3 3.1 %fusion.27 = f32[3,4,4,128,322]{3,4,2,1,0:T(8,128)S(1)} fusion(bf16[6,6,512,320]{2,3,1,0:T(8,128)(2,1)S(1)} %copy-done, bf16[3,3,3,128,512]{4,3,2,1,0:T(8,128)(2,1)S(1)} %copy-done.1), kind=kOutput, calls=%fused_computation.27 | convolution fusion | flops 2025848832 | bytes 20103168 | tf_op jit(solution)/shard_map/kdc,frcw->kfrdw/dot_general | solution.py:28
  146.4 4.1 %fusion.30 = f32[3,4,4,128,322]{3,4,2,1,0:T(8,128)S(1)} fusion(bf16[6,6,512,320]{2,3,1,0:T(8,128)(2,1)S(1)} %copy-done, bf16[3,3,3,128,512]{4,3,2,1,0:T(8,128)(2,1)} %param.6), kind=kOutput, calls=%fused_computation.28 | convolution fusion | flops 2025848832 | bytes 20103168 | tf_op jit(solution)/shard_map/kdc,frcw->kfrdw/dot_general | solution.py:28
  150.5 6.2 %fusion.33 = f32[3,4,4,128,322]{3,4,2,1,0:T(8,128)} fusion(bf16[6,6,512,320]{2,3,1,0:T(8,128)(2,1)S(1)} %copy-done, bf16[3,3,3,128,512]{4,3,2,1,0:T(8,128)(2,1)} %param.6), kind=kOutput, calls=%fused_computation.29 | convolution fusion | flops 2025848832 | bytes 20103168 | tf_op jit(solution)/shard_map/kdc,frcw->kfrdw/dot_general | solution.py:28
  156.7 6.2 %fusion.36 = f32[3,4,4,128,322]{3,4,2,1,0:T(8,128)} fusion(bf16[6,6,512,320]{2,3,1,0:T(8,128)(2,1)S(1)} %copy-done, bf16[3,3,3,128,512]{4,3,2,1,0:T(8,128)(2,1)} %param.6), kind=kOutput, calls=%fused_computation.30 | convolution fusion | flops 2025848832 | bytes 20103168 | tf_op jit(solution)/shard_map/kdc,frcw->kfrdw/dot_general | solution.py:28
  162.9 6.1 %fusion.39 = f32[3,4,4,128,322]{3,4,0,2,1:T(8,128)} fusion(bf16[6,6,512,320]{2,3,1,0:T(8,128)(2,1)S(1)} %copy-done, bf16[3,3,3,128,512]{4,3,2,1,0:T(8,128)(2,1)} %param.6), kind=kOutput, calls=%fused_computation.31 | convolution fusion | flops 2025848832 | bytes 20103168 | tf_op jit(solution)/shard_map/kdc,frcw->kfrdw/dot_general | solution.py:28
  169.1 19.9 %fusion.56 = bf16[4,4,128,320]{2,3,1,0:T(8,128)(2,1)} fusion(f32[3,4,4,128,322]{3,4,2,1,0:T(8,128)} %fusion.36, f32[3,4,4,128,322]{3,4,2,1,0:T(8,128)} %fusion.33, f32[3,4,4,128,322]{3,4,2,1,0:T(8,128)S(1)} %fusion.30, f32[3,4,4,128,322]{3,4,2,1,0:T(8,128)S(1)} %fusion.27, f32[3,4,4,128,322]{3,4,0,2,1:T(8,128)} %fusion.51, ...), kind=kLoop, calls=%fused_computation.40 | loop fusion | flops 18350080 | bytes 72090112 | tf_op jit(solution)/shard_map/convert_element_type | solution.py:51
  (3 shorter events, 0.0 us)
Async XLA Ops:
  6.5 112.1 %all-gather.2.cloned.1.call-start = ((), (), s32[]{:S(2)}) async-start(), calls=%async_computation | async-start | bytes 14745600 | tf_op jit(solution)/shard_map/all_gather | solution.py:50
  9.2 25.9 %collective-permute-start = (bf16[6,1,128,320]{2,3,1,0:T(8,128)(2,1)S(1)}, bf16[6,1,128,320]{2,3,1,0:T(8,128)(2,1)S(1)}, u32[]{:S(2)}, u32[]{:S(2)}) collective-permute-start(bf16[6,1,128,320]{2,3,1,0:T(8,128)(2,1)S(1)} %get-tuple-element.5), channel_id=1, source_target_pairs={{0,4},{4,8},{8,12},{12,16},{16,20},{20,24},{24,28},{1,5},{5,9},{9,... | collective-permute-start | bytes 1474568 | tf_op jit(solution)/shard_map/ppermute | solution.py:12
  14.2 104.5 %copy-start.1 = (bf16[3,3,3,128,512]{4,3,2,1,0:T(8,128)(2,1)S(1)}, bf16[3,3,3,128,512]{4,3,2,1,0:T(8,128)(2,1)}, u32[]{:S(2)}) copy-start(bf16[3,3,3,128,512]{4,3,2,1,0:T(8,128)(2,1)} %param.6) | copy-start | bytes 10616836
  14.2 21.0 %collective-permute-start.1 = (bf16[6,1,128,320]{2,3,1,0:T(8,128)(2,1)S(1)}, bf16[6,1,128,320]{2,3,1,0:T(8,128)(2,1)S(1)}, u32[]{:S(2)}, u32[]{:S(2)}) collective-permute-start(bf16[6,1,128,320]{2,3,1,0:T(8,128)(2,1)S(1)} %get-tuple-element.6), channel_id=1, source_target_pairs={{4,0},{8,4},{12,8},{16,12},{20,16},{24,20},{28,24},{5,1},{9,5},{13... | collective-permute-start | bytes 1474568 | tf_op jit(solution)/shard_map/ppermute | solution.py:15
  118.6 9.1 %copy-start = (bf16[6,6,512,320]{2,3,1,0:T(8,128)(2,1)S(1)}, bf16[6,6,512,320]{2,3,1,0:T(8,128)(2,1)}, u32[]{:S(2)}) copy-start(bf16[6,6,512,320]{2,3,1,0:T(8,128)(2,1)} %all-gather.2.cloned.1.call-done) | copy-start | bytes 35389444
  162.9 6.2 %copy-start.2 = (f32[128]{0:T(128)S(1)}, f32[128]{0:T(128)}, u32[]{:S(2)}) copy-start(f32[128]{0:T(128)} %param.7) | copy-start | bytes 1540
Sparse Core Ops, SparseCore 0:
  37.2 81.3 all-gather.1
where the time goes:
time: 196 us
  waiting for transfers between devices  101 us (52%)
  matrix products  50.4 us (26%)
  other arithmetic  21.8 us (11%)
  between operations  13.5 us (7%)
  starting transfers between devices  6.46 us (3%)
  local copies, waits for them, and re-layouts  2.7 us (1%)
    all_gather x1, waiting for transfers between devices, on_device(): lax.all_gather(rimmed, 'chan', axis=2, tiled=True)  81.5 us
    dot_general x9, matrix products, convolve(): jnp.einsum('kdc,frcw->kfrdw', kernel[time_tap, row_tap], window, preferre...  50.4 us
    convert_element_type x1, other arithmetic, on_device(): return (summed + out_bias[None, None, :, None]).astype(jnp.bfloat16)  19.9 us
    ppermute x1, waiting for transfers between devices, with_halo(): lax.ppermute(lax.slice_in_dim(block, block.shape[dim] - width, None, axis...  19.4 us
    ppermute x1, starting transfers between devices, with_halo(): lax.ppermute(lax.slice_in_dim(block, block.shape[dim] - width, None, axis...  4.9 us
  transfers between devices with their start and end apart: 3, of which 2 were waited for; matrix products, arithmetic and copies ran while one was open for 0% of the time, Pallas kernels for 0%

commit v1 on v0

v1 whole, which is shorter than its diff:
```python
import functools

import jax
import jax.numpy as jnp
from jax import lax
from jax.experimental import pallas as pl
from jax.experimental.pallas import tpu as pltpu
from jax.sharding import PartitionSpec as P

MESH = pl.DeviceIdType.MESH
LANES = 128
CORES = 2


def conv_kernel(
    dims, cached_ref, new_ref, w_ref, bias_ref, out_ref,
    xb, hb, wb, acc, obuf,
    local_sem, weight_sem, out_sem,
    peer_send, peer_recv, sib_send, sib_recv,
    edge_send, edge_recv, fwd_send, fwd_recv,
):
    bands, chans, cached, outs, depth, width, row_count = dims
    frames = cached + outs
    chips = chans // CORES
    band, chan = lax.axis_index("band"), lax.axis_index("chan")
    chip, core = chan // CORES, chan % CORES
    sibling = {"chan": chip * CORES + (1 - core)}
    has_above, has_below = band > 0, band < bands - 1
    sides = ((0, has_above, {"band": band - 1}), (1, has_below, {"band": band + 1}))

    def peer(step):
        return {"chan": lax.rem(chip + step, chips) * CORES + core}

    def own(f):
        return cached_ref.at[f] if f < cached else new_ref.at[f - cached]

    def remote(src, dst, send, recv, device):
        return pltpu.make_async_remote_copy(
            src_ref=src, dst_ref=dst, send_sem=send, recv_sem=recv,
            device_id=device, device_id_type=MESH,
        )

    def weight_copy(slot, t):
        owner = lax.rem(chip + chips - slot, chips)
        span = CORES * depth
        return pltpu.make_async_copy(
            w_ref.at[t, :, pl.ds(pl.multiple_of(owner * span, LANES), span)],
            wb.at[slot, :, pl.ds(t * span, span)],
            weight_sem.at[slot, t],
        )

    def local_copy(f):
        return pltpu.make_async_copy(own(f), xb.at[0, f, core], local_sem.at[f])

    def peer_copy(step, f):
        return remote(
            own(f), xb.at[step, f, core],
            peer_send.at[step, f], peer_recv.at[step, f], peer(step),
        )

    def sib_copy(slot, f):
        src = own(f) if slot == 0 else xb.at[slot, f, core]
        return remote(
            src, xb.at[slot, f, core], sib_send.at[slot, f], sib_recv.at[slot, f], sibling
        )

    def edge_copy(slot, f, side):
        part = pl.ds(0 if side == 0 else (row_count - 1) * width, width)
        src = own(f).at[part] if slot == 0 else xb.at[slot, f, core, part]
        return remote(
            src, hb.at[slot, 1 - side, f, core],
            edge_send.at[slot, side, f], edge_recv.at[slot, 1 - side, f], sides[side][2],
        )

    def fwd_copy(slot, f, rim):
        ref = hb.at[slot, rim, f, core]
        return remote(ref, ref, fwd_send.at[slot, rim, f], fwd_recv.at[slot, rim, f], sibling)

    def each_side(act):
        for side, there, device in sides:
            pl.when(there)(functools.partial(act, side, device))

    def start_edges(slot, f):
        each_side(lambda side, _: edge_copy(slot, f, side).start())

    barrier = pltpu.get_barrier_semaphore()

    def greet(device):
        pl.semaphore_signal(barrier, inc=1, device_id=device, device_id_type=MESH)

    greet(sibling)
    for step in range(1, chips):
        greet(peer(step))
    each_side(lambda _, device: greet(device))
    for slot in range(chips):
        for t in range(3):
            weight_copy(slot, t).start()
    for f in range(frames):
        local_copy(f).start()
    pl.semaphore_wait(barrier, chips + has_above.astype(jnp.int32) + has_below.astype(jnp.int32))

    ahead = 2
    for f in range(ahead):
        for step in range(1, chips):
            peer_copy(step, f).start()
    for f in range(frames):
        sib_copy(0, f).start()
    for f in range(frames):
        start_edges(0, f)

    for rim, there, _ in sides:
        @pl.when(jnp.logical_not(there))
        def _(rim=rim):
            hb[:, rim] = jnp.zeros((hb.shape[0],) + hb.shape[2:], hb.dtype)

    @pl.loop(0, outs * row_count)
    def _(n):
        at = pl.ds(pl.multiple_of(n * width, width), width)
        for j in range(3):
            start = bias_ref[...] if j == 1 else jnp.zeros_like(bias_ref)
            acc[at, j * depth : (j + 1) * depth] = jnp.broadcast_to(start, (width, depth))

    def serve(f):
        for step in range(1, chips):
            peer_copy(step, f).wait_recv()
            sib_copy(step, f).start()
            start_edges(step, f)
            peer_copy(step, f).wait_send()
            if f + ahead < frames:
                peer_copy(step, f + ahead).start()

    def serve_edges(slot, f):
        def act(rim, _):
            edge_copy(slot, f, 1 - rim).wait_recv()
            fwd_copy(slot, f, rim).start()

        each_side(act)

    def wait_rims(slot, f):
        each_side(lambda rim, _: fwd_copy(slot, f, rim).wait_recv())

    def add(slot, f, pieces, row, taps):
        lo, hi = taps
        group = 3 * depth
        product = lax.dot_general(
            jnp.concatenate(pieces, axis=1),
            wb[slot, lo * group : (hi + 1) * group, :],
            (((1,), (1,)), ((), ())),
            preferred_element_type=jnp.float32,
        )
        for i in range(lo, hi + 1):
            start = (f * row_count + row + 1 - i) * width
            at = pl.ds(start if isinstance(row, int) else pl.multiple_of(start, width), width)
            acc[at, :] = acc[at, :] + product[:, (i - lo) * group : (i - lo + 1) * group]

    def accumulate(slot, f):
        def add_row(row, taps):
            start = row * width
            at = pl.ds(start if isinstance(row, int) else pl.multiple_of(start, width), width)
            add(
                slot, f, [xb[slot, f + t, c, at, :] for t in range(3) for c in range(CORES)],
                row, taps,
            )

        add_row(0, (0, 1))
        add_row(row_count - 1, (1, 2))
        pl.loop(1, row_count - 1)(lambda row: add_row(row, (0, 2)))

    def accumulate_rims(slot, f):
        for rim, row in ((0, -1), (1, row_count)):
            add(
                slot, f, [hb[slot, rim, f + t, c] for t in range(3) for c in range(CORES)],
                row, (2 * rim, 2 * rim),
            )

    def finish(f):
        column = lax.broadcasted_iota(jnp.int32, (width, depth), 0)

        @pl.loop(0, row_count)
        def _(row):
            at = pl.ds(pl.multiple_of((f * row_count + row) * width, width), width)
            left = pltpu.roll(acc[at, 0:depth], 1, 0)
            right = pltpu.roll(acc[at, 2 * depth : 3 * depth], width - 1, 0)
            total = acc[at, depth : 2 * depth]
            total = total + jnp.where(column == 0, 0.0, left)
            total = total + jnp.where(column == width - 1, 0.0, right)
            obuf[f, pl.ds(pl.multiple_of(row * width, width), width), :] = total.astype(obuf.dtype)

        out_copy(f).start()

    def out_copy(f):
        return pltpu.make_async_copy(obuf.at[f], out_ref.at[f], out_sem.at[f])

    for t in range(3):
        weight_copy(0, t).wait()
    for f in range(outs):
        for g in range(3) if f == 0 else (f + 2,):
            local_copy(g).wait()
            sib_copy(0, g).wait_recv()
        accumulate(0, f)
    for slot in range(1, chips):
        for t in range(3):
            weight_copy(slot, t).wait()

    serve(0)
    serve(1)
    for f in range(frames):
        serve_edges(0, f)
    for f in range(2, frames):
        serve(f)
        for step in range(1, chips):
            for g in (0, 1) if f == 2 else (f - 1,):
                serve_edges(step, g)
            for g in (0, 1, 2) if f == 2 else (f,):
                sib_copy(step, g).wait_recv()
            accumulate(step, f - 2)
        if f == 3:
            for g in range(frames):
                wait_rims(0, g)
            for o in range(outs):
                accumulate_rims(0, o)
        if f >= 3:
            for step in range(1, chips):
                for g in (0, 1, 2) if f == 3 else (f - 1,):
                    wait_rims(step, g)
                accumulate_rims(step, f - 3)
            finish(f - 3)
    for step in range(1, chips):
        serve_edges(step, frames - 1)
        wait_rims(step, frames - 1)
        accumulate_rims(step, outs - 1)
    finish(outs - 1)

    for f in range(frames):
        for slot in range(chips):
            sib_copy(slot, f).wait_send()

            def gone(side, _, slot=slot, f=f):
                edge_copy(slot, f, side).wait_send()
                fwd_copy(slot, f, side).wait_send()

            each_side(gone)
    for f in range(outs):
        out_copy(f).wait()


def on_device(bands, chans, new_frames, cached_frames, conv_weight, out_bias):
    outs, row_count, own_depth, width = new_frames.shape
    cached = cached_frames.shape[0]
    frames = cached + outs
    chips = chans // CORES
    depth = -(-own_depth // LANES) * LANES
    extra = depth - own_depth

    def rows_first(block):
        block = block.transpose(0, 1, 3, 2).reshape(block.shape[0], row_count * width, own_depth)
        return jnp.pad(block, ((0, 0), (0, 0), (0, extra)))

    weights = conv_weight.reshape(3, 9, own_depth, chans, own_depth)
    weights = jnp.pad(weights, ((0, 0), (0, 0), (0, extra), (0, 0), (0, extra)))
    weights = weights.reshape(3, 9 * depth, chans * depth)
    dims = (bands, chans, cached, outs, depth, width, row_count)
    sem = pltpu.SemaphoreType.DMA
    positions = row_count * width
    result = pl.pallas_call(
        functools.partial(conv_kernel, dims),
        out_shape=jax.ShapeDtypeStruct((outs, positions, depth), jnp.bfloat16),
        in_specs=[
            pl.BlockSpec(memory_space=pl.ANY),
            pl.BlockSpec(memory_space=pl.ANY),
            pl.BlockSpec(memory_space=pl.ANY),
            pl.BlockSpec(memory_space=pltpu.VMEM),
        ],
        out_specs=pl.BlockSpec(memory_space=pl.ANY),
        scratch_shapes=[
            pltpu.VMEM((chips, frames, CORES, positions, depth), jnp.bfloat16),
            pltpu.VMEM((chips, 2, frames, CORES, width, depth), jnp.bfloat16),
            pltpu.VMEM((chips, 9 * depth, 3 * CORES * depth), jnp.bfloat16),
            pltpu.VMEM((outs * positions, 3 * depth), jnp.float32),
            pltpu.VMEM((outs, positions, depth), jnp.bfloat16),
            sem((frames,)),
            sem((chips, 3)),
            sem((outs,)),
            sem((chips, frames)),
            sem((chips, frames)),
            sem((chips, frames)),
            sem((chips, frames)),
            sem((chips, 2, frames)),
            sem((chips, 2, frames)),
            sem((chips, 2, frames)),
            sem((chips, 2, frames)),
        ],
        compiler_params=pltpu.CompilerParams(
            collective_id=0, has_side_effects=True, vmem_limit_bytes=56 * 2**20
        ),
        cost_estimate=pl.CostEstimate(
            flops=2 * 27 * outs * positions * depth * chans * depth,
            bytes_accessed=2 * (weights.size + (frames + outs) * positions * depth),
            transcendentals=0,
        ),
    )(
        rows_first(cached_frames), rows_first(new_frames), weights,
        jnp.pad(out_bias, (0, extra))[None, :],
    )
    result = result[:, :, :own_depth].reshape(outs, row_count, width, own_depth)
    return result.transpose(0, 1, 3, 2)


def solution(mesh):
    in_specs = (
        P(None, "band", "chan", None),
        P(None, "band", "chan", None),
        P(None, None, None, "chan", None),
        P("chan"),
    )
    out_specs = P(None, "band", "chan", None)
    return jax.shard_map(
        functools.partial(on_device, mesh.shape["band"], mesh.shape["chan"]),
        mesh=mesh, in_specs=in_specs, out_specs=out_specs, check_vma=False,
    )
```

time: 196 us -> 61.1 us (0.31)
  waiting for transfers between devices: 101 us -> 0 us
  Pallas kernels: 0 us -> 57.6 us
  matrix products: 50.4 us -> 0 us
  other arithmetic: 21.8 us -> 0 us
  between operations: 13.5 us -> 0.01 us
  starting transfers between devices: 6.46 us -> 0 us
    all_gather x1 -> x0, waiting for transfers between devices: 81.5 us -> none  [on_device(): lax.all_gather(rimmed, 'chan', axis=2, tiled=True)]
    pallas_call x0 -> x1, Pallas kernels: none -> 57.6 us  [on_device(): pl.pallas_call(functools.partial(conv_kernel, dims), out_shape=jax.ShapeD...]
    dot_general x9 -> x0, matrix products: 50.4 us -> none  [convolve(): jnp.einsum('kdc,frcw->kfrdw', kernel[time_tap, row_tap], window, preferre...]
    convert_element_type x1 -> x0, other arithmetic: 19.9 us -> none  [on_device(): return (summed + out_bias[None, None, :, None]).astype(jnp.bfloat16)]
    ppermute x2 -> x0, waiting for transfers between devices: 19.4 us -> none  [the longest x1 19.4 us: with_halo(): lax.ppermute(lax.slice_in_dim(block, block.shape[dim] - width, None, axis...]
    ppermute x2 -> x0, starting transfers between devices: 6.46 us -> none  [the longest x1 4.9 us: with_halo(): lax.ppermute(lax.slice_in_dim(block, block.shape[dim] - width, None, axis...]
  transfers between devices with their start and end apart: 3 -> 0, of which waited for: 2 -> 0; matrix products, arithmetic and copies ran while one was open for 0% -> 0% of each run, Pallas kernels for 0% -> 0%
where the time goes in v1:
time: 61.1 us; the launch traced here: 60.1 us
  Pallas kernels  57.6 us (94%)
  local copies, waits for them, and re-layouts  2.47 us (4%)
    pallas_call x1, Pallas kernels, on_device(): pl.pallas_call(functools.partial(conv_kernel, dims), out_shape=jax.ShapeD...  57.6 us
    unnamed x1, local copies, waits for them, and re-layouts  2.47 us

profile of v1, /device:TPU:0, one launch (start us, length us, event | category | flops | bytes accessed | tf_op | source)
XLA Modules:
  0.0 60.1 jit_solution(15881971856044335665)
XLA Ops:
  0.0 57.6 %shard_map.46 = bf16[4,1280,128]{2,1,0:T(8,128)(2,1)} custom-call(bf16[2,1280,128]{2,1,0:T(8,128)(2,1)} %bitcast.14, bf16[4,1280,128]{2,1,0:T(8,128)(2,1)} %bitcast.13, bf16[3,1152,512]{2,1,0:T(8,128)(2,1)} %bitcast.12, f32[1,128]{1,0:T(1,128)} %bitcast.15), custom_call_target="tpu_custom_call" | custom-call | flops 18119393280 | bytes 6815744 | tf_op jit(solution)/shard_map/pallas_call | solution.py:265
  57.6 2.5 %copy.6 = bf16[4,4,128,320]{2,3,1,0:T(8,128)(2,1)} copy(bf16[4,4,128,320]{2,3,1,0:T(8,128)(2,1)} %bitcast.11) | data formatting | bytes 2621440

commit v2 on v1

--- a/solution.py
+++ b/solution.py
@@ -52,21 +52,31 @@
     def local_copy(f):
         return pltpu.make_async_copy(own(f), xb.at[0, f, core], local_sem.at[f])
 
-    def peer_copy(step, f):
+    FIRST, LAST, MIDDLE = range(3)
+    spans = (
+        pl.ds(0, width),
+        pl.ds((row_count - 1) * width, width),
+        pl.ds(width, (row_count - 2) * width),
+    )
+
+    def peer_copy(step, f, part):
         return remote(
-            own(f), xb.at[step, f, core],
-            peer_send.at[step, f], peer_recv.at[step, f], peer(step),
-        )
-
-    def sib_copy(slot, f):
-        src = own(f) if slot == 0 else xb.at[slot, f, core]
+            own(f).at[spans[part]], xb.at[step, f, core, spans[part]],
+            peer_send.at[step, part, f], peer_recv.at[step, part, f], peer(step),
+        )
+
+    def own_copy(f):
         return remote(
-            src, xb.at[slot, f, core], sib_send.at[slot, f], sib_recv.at[slot, f], sibling
-        )
+            own(f), xb.at[0, f, core], sib_send.at[0, 0, f], sib_recv.at[0, 0, f], sibling
+        )
+
+    def sib_copy(step, f, part):
+        ref = xb.at[step, f, core, spans[part]]
+        return remote(ref, ref, sib_send.at[step, part, f], sib_recv.at[step, part, f], sibling)
 
     def edge_copy(slot, f, side):
-        part = pl.ds(0 if side == 0 else (row_count - 1) * width, width)
-        src = own(f).at[part] if slot == 0 else xb.at[slot, f, core, part]
+        span = spans[FIRST if side == 0 else LAST]
+        src = own(f).at[span] if slot == 0 else xb.at[slot, f, core, span]
         return remote(
             src, hb.at[slot, 1 - side, f, core],
             edge_send.at[slot, side, f], edge_recv.at[slot, 1 - side, f], sides[side][2],
@@ -99,12 +109,19 @@
         local_copy(f).start()
     pl.semaphore_wait(barrier, chips + has_above.astype(jnp.int32) + has_below.astype(jnp.int32))
 
-    ahead = 2
-    for f in range(ahead):
+    ahead = 4
+    queue = [(f, (FIRST, LAST)) for f in range(frames)] + [(f, (MIDDLE,)) for f in range(frames)]
+
+    def send(place):
+        f, parts = queue[place]
         for step in range(1, chips):
-            peer_copy(step, f).start()
-    for f in range(frames):
-        sib_copy(0, f).start()
+            for part in parts:
+                peer_copy(step, f, part).start()
+
+    for place in range(ahead):
+        send(place)
+    for f in range(frames):
+        own_copy(f).start()
     for f in range(frames):
         start_edges(0, f)
 
@@ -120,14 +137,19 @@
             start = bias_ref[...] if j == 1 else jnp.zeros_like(bias_ref)
             acc[at, j * depth : (j + 1) * depth] = jnp.broadcast_to(start, (width, depth))
 
-    def serve(f):
+    def serve(place):
+        f, parts = queue[place]
         for step in range(1, chips):
-            peer_copy(step, f).wait_recv()
-            sib_copy(step, f).start()
-            start_edges(step, f)
-            peer_copy(step, f).wait_send()
-            if f + ahead < frames:
-                peer_copy(step, f + ahead).start()
+            for part in parts:
+                peer_copy(step, f, part).wait_recv()
+                sib_copy(step, f, part).start()
+            if FIRST in parts:
+                start_edges(step, f)
+        for step in range(1, chips):
+            for part in parts:
+                peer_copy(step, f, part).wait_send()
+        if place + ahead < len(queue):
+            send(place + ahead)
 
     def serve_edges(slot, f):
         def act(rim, _):
@@ -139,12 +161,12 @@
     def wait_rims(slot, f):
         each_side(lambda rim, _: fwd_copy(slot, f, rim).wait_recv())
 
-    def add(slot, f, pieces, row, taps):
+    def add(slot, f, ref_of, times, row, taps):
         lo, hi = taps
-        group = 3 * depth
+        group, span = 3 * depth, CORES * depth
         product = lax.dot_general(
-            jnp.concatenate(pieces, axis=1),
-            wb[slot, lo * group : (hi + 1) * group, :],
+            jnp.concatenate([ref_of(f + t, c) for t in times for c in range(CORES)], axis=1),
+            wb[slot, lo * group : (hi + 1) * group, times[0] * span : (times[-1] + 1) * span],
             (((1,), (1,)), ((), ())),
             preferred_element_type=jnp.float32,
         )
@@ -153,23 +175,24 @@
             at = pl.ds(start if isinstance(row, int) else pl.multiple_of(start, width), width)
             acc[at, :] = acc[at, :] + product[:, (i - lo) * group : (i - lo + 1) * group]
 
-    def accumulate(slot, f):
-        def add_row(row, taps):
-            start = row * width
-            at = pl.ds(start if isinstance(row, int) else pl.multiple_of(start, width), width)
-            add(
-                slot, f, [xb[slot, f + t, c, at, :] for t in range(3) for c in range(CORES)],
-                row, taps,
-            )
-
-        add_row(0, (0, 1))
-        add_row(row_count - 1, (1, 2))
-        pl.loop(1, row_count - 1)(lambda row: add_row(row, (0, 2)))
-
-    def accumulate_rims(slot, f):
+    every = (0, 1, 2)
+
+    def add_row(slot, f, row, taps, times=every):
+        start = row * width
+        at = pl.ds(start if isinstance(row, int) else pl.multiple_of(start, width), width)
+        add(slot, f, lambda g, c: xb[slot, g, c, at, :], times, row, taps)
+
+    def add_edges(slot, f):
+        add_row(slot, f, 0, (0, 1))
+        add_row(slot, f, row_count - 1, (1, 2))
+
+    def add_middle(slot, f, times=every):
+        pl.loop(1, row_count - 1)(lambda row: add_row(slot, f, row, (0, 2), times))
+
+    def add_rims(slot, f, times=every):
         for rim, row in ((0, -1), (1, row_count)):
             add(
-                slot, f, [hb[slot, rim, f + t, c] for t in range(3) for c in range(CORES)],
+                slot, f, lambda g, c, rim=rim: hb[slot, rim, g, c], times,
                 row, (2 * rim, 2 * rim),
             )
 
@@ -191,49 +214,63 @@
     def out_copy(f):
         return pltpu.make_async_copy(obuf.at[f], out_ref.at[f], out_sem.at[f])
 
+    others = range(1, chips)
+
+    def wait_sibling(f, parts):
+        for step in others:
+            for part in parts:
+                sib_copy(step, f, part).wait_recv()
+
     for t in range(3):
         weight_copy(0, t).wait()
     for f in range(outs):
         for g in range(3) if f == 0 else (f + 2,):
             local_copy(g).wait()
-            sib_copy(0, g).wait_recv()
-        accumulate(0, f)
-    for slot in range(1, chips):
+            own_copy(g).wait_recv()
+        add_edges(0, f)
+        add_middle(0, f)
+        serve(f)
+    for slot in others:
         for t in range(3):
             weight_copy(slot, t).wait()
-
-    serve(0)
-    serve(1)
+    for place in range(outs, frames):
+        serve(place)
     for f in range(frames):
         serve_edges(0, f)
+        wait_sibling(f, (FIRST, LAST))
+    for f in range(outs):
+        for step in others:
+            add_edges(step, f)
+        if f % 2 == 1:
+            serve(frames + f // 2)
+    for f in range(frames):
+        wait_rims(0, f)
+    for f in range(outs):
+        add_rims(0, f)
     for f in range(2, frames):
-        serve(f)
-        for step in range(1, chips):
-            for g in (0, 1) if f == 2 else (f - 1,):
+        serve(frames + f)
+        last = f == frames - 1
+        for step in others:
+            for g in (0, 1, 2) if f == 2 else (f,):
                 serve_edges(step, g)
+        for g in (0, 1, 2) if f == 2 else (f,):
+            wait_sibling(g, (MIDDLE,))
+        for step in others:
+            add_middle(step, f - 2, (2,) if last else every)
             for g in (0, 1, 2) if f == 2 else (f,):
-                sib_copy(step, g).wait_recv()
-            accumulate(step, f - 2)
-        if f == 3:
-            for g in range(frames):
-                wait_rims(0, g)
-            for o in range(outs):
-                accumulate_rims(0, o)
-        if f >= 3:
-            for step in range(1, chips):
-                for g in (0, 1, 2) if f == 3 else (f - 1,):
-                    wait_rims(step, g)
-                accumulate_rims(step, f - 3)
-            finish(f - 3)
-    for step in range(1, chips):
-        serve_edges(step, frames - 1)
-        wait_rims(step, frames - 1)
-        accumulate_rims(step, outs - 1)
-    finish(outs - 1)
-
-    for f in range(frames):
+                wait_rims(step, g)
+            add_rims(step, f - 2, (2,) if last else every)
+        finish(f - 2)
+        if f == frames - 2:
+            for step in others:
+                add_middle(step, outs - 1, (0, 1))
+                add_rims(step, outs - 1, (0, 1))
+
+    for f in range(frames):
+        own_copy(f).wait_send()
         for slot in range(chips):
-            sib_copy(slot, f).wait_send()
+            for part in range(3) if slot > 0 else ():
+                sib_copy(slot, f, part).wait_send()
 
             def gone(side, _, slot=slot, f=f):
                 edge_copy(slot, f, side).wait_send()
@@ -281,10 +318,10 @@
             sem((frames,)),
             sem((chips, 3)),
             sem((outs,)),
-            sem((chips, frames)),
-            sem((chips, frames)),
-            sem((chips, frames)),
-            sem((chips, frames)),
+            sem((chips, 3, frames)),
+            sem((chips, 3, frames)),
+            sem((chips, 3, frames)),
+            sem((chips, 3, frames)),
             sem((chips, 2, frames)),
             sem((chips, 2, frames)),
             sem((chips, 2, frames)),

time: 61.1 us -> 62.7 us (1.026)
  the two profiles are of different devices: /device:TPU:0 before, /device:TPU:6 now
where the time goes in v2:
time: 62.7 us; the launch traced here: 62.5 us
  Pallas kernels  60 us (96%)
  local copies, waits for them, and re-layouts  2.47 us (4%)
    pallas_call x1, Pallas kernels, on_device(): pl.pallas_call(functools.partial(conv_kernel, dims), out_shape=jax.ShapeD...  60 us
    unnamed x1, local copies, waits for them, and re-layouts  2.47 us

profile of v2, /device:TPU:6, one launch (start us, length us, event | category | flops | bytes accessed | tf_op | source)
XLA Modules:
  0.0 62.5 jit_solution(16840648091998388436)
XLA Ops:
  0.0 60.0 %shard_map.46 = bf16[4,1280,128]{2,1,0:T(8,128)(2,1)} custom-call(bf16[2,1280,128]{2,1,0:T(8,128)(2,1)} %bitcast.14, bf16[4,1280,128]{2,1,0:T(8,128)(2,1)} %bitcast.13, bf16[3,1152,512]{2,1,0:T(8,128)(2,1)} %bitcast.12, f32[1,128]{1,0:T(1,128)} %bitcast.15), custom_call_target="tpu_custom_call" | custom-call | flops 18119393280 | bytes 6815744 | tf_op jit(solution)/shard_map/pallas_call | solution.py:302
  60.1 2.5 %copy.6 = bf16[4,4,128,320]{2,3,1,0:T(8,128)(2,1)} copy(bf16[4,4,128,320]{2,3,1,0:T(8,128)(2,1)} %bitcast.11) | data formatting | bytes 2621440

commit v3 on v2

--- a/solution.py
+++ b/solution.py
@@ -14,7 +14,7 @@
 
 def conv_kernel(
     dims, cached_ref, new_ref, w_ref, bias_ref, out_ref,
-    xb, hb, wb, acc, obuf,
+    xb, hb, wb, wt, acc, obuf,
     local_sem, weight_sem, out_sem,
     peer_send, peer_recv, sib_send, sib_recv,
     edge_send, edge_recv, fwd_send, fwd_recv,
@@ -30,6 +30,15 @@
 
     def peer(step):
         return {"chan": lax.rem(chip + step, chips) * CORES + core}
+
+    def turn_weights(slot):
+        for t in range(3):
+            weight_copy(slot, t).wait()
+
+        @pl.loop(0, 9)
+        def _(n):
+            at = pl.ds(pl.multiple_of(n * depth, depth), depth)
+            wt[slot, :, at] = wb[slot, at, :].T
 
     def own(f):
         return cached_ref.at[f] if f < cached else new_ref.at[f - cached]
@@ -166,8 +175,8 @@
         group, span = 3 * depth, CORES * depth
         product = lax.dot_general(
             jnp.concatenate([ref_of(f + t, c) for t in times for c in range(CORES)], axis=1),
-            wb[slot, lo * group : (hi + 1) * group, times[0] * span : (times[-1] + 1) * span],
-            (((1,), (1,)), ((), ())),
+            wt[slot, times[0] * span : (times[-1] + 1) * span, lo * group : (hi + 1) * group],
+            (((1,), (0,)), ((), ())),
             preferred_element_type=jnp.float32,
         )
         for i in range(lo, hi + 1):
@@ -221,8 +230,7 @@
             for part in parts:
                 sib_copy(step, f, part).wait_recv()
 
-    for t in range(3):
-        weight_copy(0, t).wait()
+    turn_weights(0)
     for f in range(outs):
         for g in range(3) if f == 0 else (f + 2,):
             local_copy(g).wait()
@@ -231,8 +239,7 @@
         add_middle(0, f)
         serve(f)
     for slot in others:
-        for t in range(3):
-            weight_copy(slot, t).wait()
+        turn_weights(slot)
     for place in range(outs, frames):
         serve(place)
     for f in range(frames):
@@ -281,6 +288,17 @@
         out_copy(f).wait()
 
 
+def copy_kernel(src_ref, dst_ref, sems):
+    copies = [
+        pltpu.make_async_copy(src_ref.at[f], dst_ref.at[f], sems.at[f])
+        for f in range(src_ref.shape[0])
+    ]
+    for copy in copies:
+        copy.start()
+    for copy in copies:
+        copy.wait()
+
+
 def on_device(bands, chans, new_frames, cached_frames, conv_weight, out_bias):
     outs, row_count, own_depth, width = new_frames.shape
     cached = cached_frames.shape[0]
@@ -313,6 +331,7 @@
             pltpu.VMEM((chips, frames, CORES, positions, depth), jnp.bfloat16),
             pltpu.VMEM((chips, 2, frames, CORES, width, depth), jnp.bfloat16),
             pltpu.VMEM((chips, 9 * depth, 3 * CORES * depth), jnp.bfloat16),
+            pltpu.VMEM((chips, 3 * CORES * depth, 9 * depth), jnp.bfloat16),
             pltpu.VMEM((outs * positions, 3 * depth), jnp.float32),
             pltpu.VMEM((outs, positions, depth), jnp.bfloat16),
             sem((frames,)),
@@ -339,6 +358,16 @@
         rows_first(cached_frames), rows_first(new_frames), weights,
         jnp.pad(out_bias, (0, extra))[None, :],
     )
+    result = pl.pallas_call(
+        copy_kernel,
+        out_shape=jax.ShapeDtypeStruct(result.shape, result.dtype),
+        in_specs=[pl.BlockSpec(memory_space=pl.ANY)],
+        out_specs=pl.BlockSpec(memory_space=pl.ANY),
+        scratch_shapes=[sem((outs,))],
+        cost_estimate=pl.CostEstimate(
+            flops=0, bytes_accessed=4 * result.size, transcendentals=0
+        ),
+    )(result)
     result = result[:, :, :own_depth].reshape(outs, row_count, width, own_depth)
     return result.transpose(0, 1, 3, 2)
 

time: 62.7 us -> 101 us (1.61)
  the two profiles are of different devices: /device:TPU:6 before, /device:TPU:20 now
where the time goes in v3:
time: 101 us
  Pallas kernels  100 us (99%)
    pallas_call x1, Pallas kernels, on_device(): pl.pallas_call(functools.partial(conv_kernel, dims), out_shape=jax.ShapeD...  59.7 us
    pallas_call x1, Pallas kernels, on_device(): pl.pallas_call(copy_kernel, out_shape=jax.ShapeDtypeStruct(result.shape,...  40.8 us

profile of v3, /device:TPU:20, one launch (start us, length us, event | category | flops | bytes accessed | tf_op | source)
XLA Modules:
  0.0 100.7 jit_solution(524181621069052440)
XLA Ops:
  0.0 59.7 %shard_map.46.src_ref = bf16[4,1280,128]{2,1,0:T(8,128)(2,1)} custom-call(bf16[2,1280,128]{2,1,0:T(8,128)(2,1)} %bitcast.13, bf16[4,1280,128]{2,1,0:T(8,128)(2,1)} %bitcast.12, bf16[3,1152,512]{2,1,0:T(8,128)(2,1)} %bitcast.11, f32[1,128]{1,0:T(1,128)} %bitcast.14), custom_call_target="tpu_custom_call" | custom-call | flops 18119393280 | bytes 6815744 | tf_op jit(solution)/shard_map/pallas_call | solution.py:320
  59.7 40.8 %shard_map.47 = bf16[4,1280,128]{2,1,0:T(8,128)(2,1)} custom-call(bf16[4,1280,128]{2,1,0:T(8,128)(2,1)} %shard_map.46.src_ref), custom_call_target="tpu_custom_call" | custom-call | bytes 2621440 | tf_op jit(solution)/shard_map/pallas_call | solution.py:361

commit v4 on v2

v4 whole, which is shorter than its diff:
```python
import functools

import jax
import jax.numpy as jnp
from jax import lax
from jax.experimental import pallas as pl
from jax.experimental.pallas import tpu as pltpu
from jax.sharding import PartitionSpec as P

MESH = pl.DeviceIdType.MESH
LANES = 128
CORES = 2


def conv_kernel(
    dims, cached_ref, new_ref, w_ref, bias_ref, out_ref,
    xb, wb, wt, acc, rim_out, rim_in, obuf,
    local_sem, weight_sem, out_sem,
    peer_send, peer_recv, sib_send, sib_recv,
    rim_send, rim_recv,
):
    bands, chans, cached, outs, depth, width, row_count = dims
    frames = cached + outs
    chips = chans // CORES
    band, chan = lax.axis_index("band"), lax.axis_index("chan")
    chip, core = chan // CORES, chan % CORES
    sibling = {"chan": chip * CORES + (1 - core)}
    has_above, has_below = band > 0, band < bands - 1
    sides = ((0, has_above, {"band": band - 1}), (1, has_below, {"band": band + 1}))

    def peer(step):
        return {"chan": lax.rem(chip + step, chips) * CORES + core}

    def turn_weights(slot):
        for t in range(3):
            weight_copy(slot, t).wait()

        @pl.loop(0, 9)
        def _(n):
            at = pl.ds(pl.multiple_of(n * depth, depth), depth)
            wt[slot, :, at] = wb[slot, at, :].T

    def own(f):
        return cached_ref.at[f] if f < cached else new_ref.at[f - cached]

    def remote(src, dst, send, recv, device):
        return pltpu.make_async_remote_copy(
            src_ref=src, dst_ref=dst, send_sem=send, recv_sem=recv,
            device_id=device, device_id_type=MESH,
        )

    def weight_copy(slot, t):
        owner = lax.rem(chip + chips - slot, chips)
        span = CORES * depth
        return pltpu.make_async_copy(
            w_ref.at[t, :, pl.ds(pl.multiple_of(owner * span, LANES), span)],
            wb.at[slot, :, pl.ds(t * span, span)],
            weight_sem.at[slot, t],
        )

    def local_copy(f):
        return pltpu.make_async_copy(own(f), xb.at[0, f, core], local_sem.at[f])

    FIRST, LAST, MIDDLE = range(3)
    spans = (
        pl.ds(0, width),
        pl.ds((row_count - 1) * width, width),
        pl.ds(width, (row_count - 2) * width),
    )

    def peer_copy(step, f, part):
        return remote(
            own(f).at[spans[part]], xb.at[step, f, core, spans[part]],
            peer_send.at[step, part, f], peer_recv.at[step, part, f], peer(step),
        )

    def own_copy(f):
        return remote(
            own(f), xb.at[0, f, core], sib_send.at[0, 0, f], sib_recv.at[0, 0, f], sibling
        )

    def sib_copy(step, f, part):
        ref = xb.at[step, f, core, spans[part]]
        return remote(ref, ref, sib_send.at[step, part, f], sib_recv.at[step, part, f], sibling)

    def rim_copy(f, side):
        return remote(
            rim_out.at[side, f], rim_in.at[1 - side, f],
            rim_send.at[side, f], rim_recv.at[1 - side, f], sides[side][2],
        )

    def each_side(act):
        for side, there, device in sides:
            pl.when(there)(functools.partial(act, side, device))

    barrier = pltpu.get_barrier_semaphore()

    def greet(device):
        pl.semaphore_signal(barrier, inc=1, device_id=device, device_id_type=MESH)

    greet(sibling)
    for step in range(1, chips):
        greet(peer(step))
    each_side(lambda _, device: greet(device))
    for slot in range(chips):
        for t in range(3):
            weight_copy(slot, t).start()
    for f in range(frames):
        local_copy(f).start()
    pl.semaphore_wait(barrier, chips + has_above.astype(jnp.int32) + has_below.astype(jnp.int32))

    ahead = 4
    queue = [(f, (FIRST, LAST)) for f in range(frames)] + [(f, (MIDDLE,)) for f in range(frames)]

    def send(place):
        f, parts = queue[place]
        for step in range(1, chips):
            for part in parts:
                peer_copy(step, f, part).start()

    for place in range(ahead):
        send(place)
    for f in range(frames):
        own_copy(f).start()
    for rim, there, _ in sides:
        @pl.when(jnp.logical_not(there))
        def _(rim=rim):
            rim_in[rim] = jnp.zeros(rim_in.shape[1:], rim_in.dtype)

    sum_rows = row_count + 2

    @pl.loop(0, outs * sum_rows)
    def _(n):
        at = pl.ds(pl.multiple_of(n * width, width), width)
        acc[at, :] = jnp.zeros((width, 3 * depth), acc.dtype)

    def serve(place):
        f, parts = queue[place]
        for step in range(1, chips):
            for part in parts:
                peer_copy(step, f, part).wait_recv()
                sib_copy(step, f, part).start()
        for step in range(1, chips):
            for part in parts:
                peer_copy(step, f, part).wait_send()
        if place + ahead < len(queue):
            send(place + ahead)

    every = (0, 1, 2)

    def add_row(slot, f, row, times):
        group, span = 3 * depth, CORES * depth
        at = pl.ds(pl.multiple_of(row * width, width), width)
        product = jnp.dot(
            jnp.concatenate(
                [xb[slot, f + t, c, at, :] for t in times for c in range(CORES)], axis=1
            ),
            wt[slot, times[0] * span : (times[-1] + 1) * span, :],
            preferred_element_type=jnp.float32,
        )
        for i in range(3):
            start = (f * sum_rows + row + 2 - i) * width
            to = pl.ds(pl.multiple_of(start, width), width)
            acc[to, :] = acc[to, :] + product[:, i * group : (i + 1) * group]

    def add_edges(slot, f):
        pl.loop(0, 2)(lambda n: add_row(slot, f, n * (row_count - 1), every))

    def add_middle(slot, f, times=every):
        pl.loop(1, row_count - 1)(lambda row: add_row(slot, f, row, times))

    column = lax.broadcasted_iota(jnp.int32, (width, depth), 0)

    def row_sum(f, row):
        at = pl.ds(pl.multiple_of((f * sum_rows + row) * width, width), width)
        left = pltpu.roll(acc[at, 0:depth], 1, 0)
        right = pltpu.roll(acc[at, 2 * depth : 3 * depth], width - 1, 0)
        total = acc[at, depth : 2 * depth] + jnp.where(column == 0, 0.0, left)
        return total + jnp.where(column == width - 1, 0.0, right)

    def send_rims(f):
        def act(side, _):
            rim_out[side, f] = row_sum(f, side * (sum_rows - 1))
            rim_copy(f, side).start()

        each_side(act)

    def finish(f):
        each_side(lambda rim, _: rim_copy(f, 1 - rim).wait_recv())

        def write(row, total):
            at = pl.ds(pl.multiple_of(row * width, width), width)
            obuf[f, at, :] = (total + bias_ref[...]).astype(obuf.dtype)

        @pl.loop(0, 2)
        def _(rim):
            row = rim * (row_count - 1)
            write(row, row_sum(f, row + 1) + rim_in[rim, f])

        @pl.loop(1, row_count - 1)
        def _(row):
            write(row, row_sum(f, row + 1))

        out_copy(f).start()

    def out_copy(f):
        return pltpu.make_async_copy(obuf.at[f], out_ref.at[f], out_sem.at[f])

    others = range(1, chips)

    def wait_sibling(f, parts):
        for step in others:
            for part in parts:
                sib_copy(step, f, part).wait_recv()

    turn_weights(0)
    for f in range(outs):
        for g in range(3) if f == 0 else (f + 2,):
            local_copy(g).wait()
            own_copy(g).wait_recv()
        add_edges(0, f)
        if f % 2 == 1:
            serve(f // 2)
    for slot in others:
        turn_weights(slot)
    for f in range(outs):
        add_middle(0, f)
        serve(f + 2)
        for g in (0, 1, 2) if f == 0 else (f + 2,):
            wait_sibling(g, (FIRST, LAST))
        for step in others:
            add_edges(step, f)
        send_rims(f)
    serve(frames)
    serve(frames + 1)
    for f in range(outs):
        if f == outs - 1:
            for step in others:
                add_middle(step, f, (0, 1))
        serve(frames + f + 2)
        for g in (0, 1, 2) if f == 0 else (f + 2,):
            wait_sibling(g, (MIDDLE,))
        for step in others:
            add_middle(step, f, (2,) if f == outs - 1 else every)
        finish(f)

    for f in range(frames):
        own_copy(f).wait_send()
        for slot in range(chips):
            for part in range(3) if slot > 0 else ():
                sib_copy(slot, f, part).wait_send()
    for f in range(outs):
        each_side(lambda side, _, f=f: rim_copy(f, side).wait_send())
        out_copy(f).wait()


def on_device(bands, chans, new_frames, cached_frames, conv_weight, out_bias):
    outs, row_count, own_depth, width = new_frames.shape
    cached = cached_frames.shape[0]
    frames = cached + outs
    chips = chans // CORES
    depth = -(-own_depth // LANES) * LANES
    extra = depth - own_depth

    def rows_first(block):
        block = block.transpose(0, 1, 3, 2).reshape(block.shape[0], row_count * width, own_depth)
        return jnp.pad(block, ((0, 0), (0, 0), (0, extra)))

    weights = conv_weight.reshape(3, 9, own_depth, chans, own_depth)
    weights = jnp.pad(weights, ((0, 0), (0, 0), (0, extra), (0, 0), (0, extra)))
    weights = weights.reshape(3, 9 * depth, chans * depth)
    dims = (bands, chans, cached, outs, depth, width, row_count)
    sem = pltpu.SemaphoreType.DMA
    positions = row_count * width
    result = pl.pallas_call(
        functools.partial(conv_kernel, dims),
        out_shape=jax.ShapeDtypeStruct((outs, positions, depth), jnp.bfloat16),
        in_specs=[
            pl.BlockSpec(memory_space=pl.ANY),
            pl.BlockSpec(memory_space=pl.ANY),
            pl.BlockSpec(memory_space=pl.ANY),
            pl.BlockSpec(memory_space=pltpu.VMEM),
        ],
        out_specs=pl.BlockSpec(memory_space=pl.ANY),
        scratch_shapes=[
            pltpu.VMEM((chips, frames, CORES, positions, depth), jnp.bfloat16),
            pltpu.VMEM((chips, 9 * depth, 3 * CORES * depth), jnp.bfloat16),
            pltpu.VMEM((chips, 3 * CORES * depth, 9 * depth), jnp.bfloat16),
            pltpu.VMEM((outs * (positions + 2 * width), 3 * depth), jnp.float32),
            pltpu.VMEM((2, outs, width, depth), jnp.float32),
            pltpu.VMEM((2, outs, width, depth), jnp.float32),
            pltpu.VMEM((outs, positions, depth), jnp.bfloat16),
            sem((frames,)),
            sem((chips, 3)),
            sem((outs,)),
            sem((chips, 3, frames)),
            sem((chips, 3, frames)),
            sem((chips, 3, frames)),
            sem((chips, 3, frames)),
            sem((2, outs)),
            sem((2, outs)),
        ],
        compiler_params=pltpu.CompilerParams(
            collective_id=0, has_side_effects=True, vmem_limit_bytes=56 * 2**20
        ),
        cost_estimate=pl.CostEstimate(
            flops=2 * 27 * outs * positions * depth * chans * depth,
            bytes_accessed=2 * (weights.size + (frames + outs) * positions * depth),
            transcendentals=0,
        ),
    )(
        rows_first(cached_frames), rows_first(new_frames), weights,
        jnp.pad(out_bias, (0, extra))[None, :],
    )
    result = result[:, :, :own_depth].reshape(outs, row_count, width, own_depth)
    return result.transpose(0, 1, 3, 2)


def solution(mesh):
    in_specs = (
        P(None, "band", "chan", None),
        P(None, "band", "chan", None),
        P(None, None, None, "chan", None),
        P("chan"),
    )
    out_specs = P(None, "band", "chan", None)
    return jax.shard_map(
        functools.partial(on_device, mesh.shape["band"], mesh.shape["chan"]),
        mesh=mesh, in_specs=in_specs, out_specs=out_specs, check_vma=False,
    )
```

time: 62.7 us -> 56.7 us (0.904)
  the two profiles are of different devices: /device:TPU:6 before, /device:TPU:0 now
where the time goes in v4:
time: 56.7 us; the launch traced here: 56.6 us
  Pallas kernels  54.1 us (95%)
  local copies, waits for them, and re-layouts  2.47 us (4%)
    pallas_call x1, Pallas kernels, on_device(): pl.pallas_call(functools.partial(conv_kernel, dims), out_shape=jax.ShapeD...  54.1 us
    unnamed x1, local copies, waits for them, and re-layouts  2.47 us

profile of v4, /device:TPU:0, one launch (start us, length us, event | category | flops | bytes accessed | tf_op | source)
XLA Modules:
  0.0 56.6 jit_solution(15355396748208902235)
XLA Ops:
  0.0 54.1 %shard_map.46 = bf16[4,1280,128]{2,1,0:T(8,128)(2,1)} custom-call(bf16[2,1280,128]{2,1,0:T(8,128)(2,1)} %bitcast.14, bf16[4,1280,128]{2,1,0:T(8,128)(2,1)} %bitcast.13, bf16[3,1152,512]{2,1,0:T(8,128)(2,1)} %bitcast.12, f32[1,128]{1,0:T(1,128)} %bitcast.15), custom_call_target="tpu_custom_call" | custom-call | flops 18119393280 | bytes 6815744 | tf_op jit(solution)/shard_map/pallas_call | solution.py:275
  54.1 2.5 %copy.6 = bf16[4,4,128,320]{2,3,1,0:T(8,128)(2,1)} copy(bf16[4,4,128,320]{2,3,1,0:T(8,128)(2,1)} %bitcast.11) | data formatting | bytes 2621440

commit v5 on v4

--- a/solution.py
+++ b/solution.py
@@ -252,6 +252,10 @@
     for f in range(outs):
         each_side(lambda side, _, f=f: rim_copy(f, side).wait_send())
         out_copy(f).wait()
+
+
+def copy_kernel(src_ref, dst_ref):
+    dst_ref[...] = src_ref[...]
 
 
 def on_device(bands, chans, new_frames, cached_frames, conv_weight, out_bias):
@@ -312,6 +316,17 @@
         rows_first(cached_frames), rows_first(new_frames), weights,
         jnp.pad(out_bias, (0, extra))[None, :],
     )
+    block = pl.BlockSpec((1, positions, depth), lambda f: (f, 0, 0))
+    result = pl.pallas_call(
+        copy_kernel,
+        out_shape=jax.ShapeDtypeStruct(result.shape, result.dtype),
+        grid=(outs,),
+        in_specs=[block],
+        out_specs=block,
+        cost_estimate=pl.CostEstimate(
+            flops=0, bytes_accessed=4 * result.size, transcendentals=0
+        ),
+    )(result)
     result = result[:, :, :own_depth].reshape(outs, row_count, width, own_depth)
     return result.transpose(0, 1, 3, 2)
 

time: 56.7 us -> 57.7 us (1.018)
  Pallas kernels: 54.1 us -> 57.6 us
  local copies, waits for them, and re-layouts: 2.47 us -> 0 us
    pallas_call x0 -> x1, Pallas kernels: none -> 3.47 us  [on_device(): pl.pallas_call(copy_kernel, out_shape=jax.ShapeDtypeStruct(result.shape,...]
    unnamed x1 -> x0, local copies, waits for them, and re-layouts: 2.47 us -> none
where the time goes in v5:
time: 57.7 us; the launch traced here: 57.6 us
  Pallas kernels  57.6 us (100%)
    pallas_call x1, Pallas kernels, on_device(): pl.pallas_call(functools.partial(conv_kernel, dims), out_shape=jax.ShapeD...  54.1 us
    pallas_call x1, Pallas kernels, on_device(): pl.pallas_call(copy_kernel, out_shape=jax.ShapeDtypeStruct(result.shape,...  3.47 us

profile of v5, /device:TPU:0, one launch (start us, length us, event | category | flops | bytes accessed | tf_op | source)
XLA Modules:
  0.0 57.6 jit_solution(3830575849536120457)
XLA Ops:
  0.0 54.1 %shard_map.46.src_ref = bf16[4,1280,128]{2,1,0:T(8,128)(2,1)} custom-call(bf16[2,1280,128]{2,1,0:T(8,128)(2,1)} %bitcast.13, bf16[4,1280,128]{2,1,0:T(8,128)(2,1)} %bitcast.12, bf16[3,1152,512]{2,1,0:T(8,128)(2,1)} %bitcast.11, f32[1,128]{1,0:T(1,128)} %bitcast.14), custom_call_target="tpu_custom_call" | custom-call | flops 18119393280 | bytes 6815744 | tf_op jit(solution)/shard_map/pallas_call | solution.py:279
  54.1 3.5 %shard_map.47 = bf16[4,1280,128]{2,1,0:T(8,128)(2,1)} custom-call(bf16[4,1280,128]{2,1,0:T(8,128)(2,1)} %shard_map.46.src_ref), custom_call_target="tpu_custom_call" | custom-call | bytes 2621440 | tf_op jit(solution)/shard_map/pallas_call | solution.py:320
